TPU v7x, 32 devices: a whole 2x2x4 slice. The times are simulated.
32 devices in a mesh: stream: 4 (over z), span: 2 (over y), radial: 4 (over x, core).
Axes of the slice: x: 2, y: 2, z: 4, core: 2. Of those that a mesh axis runs over, the one named last changes fastest.
Arguments:
- velocity: float32 [3, 32, 32, 1024], P(None, 'stream', 'span', 'radial'), may hold values from -6 to 6
- probe: float32 [8192, 128], P(('stream', 'span', 'radial')), may hold values from -6 to 6
- eddy: float32 [16384, 128], P(('stream', 'span', 'radial')), may hold values from 0.2 to 2.3
- slot_row: int32 [256, 64], P(('stream', 'span', 'radial')), may hold values from -1 to 255, as said below
- row_cell: int32 [8192], P(('stream', 'span', 'radial')), may hold values from 0 to 32767
Outputs:
- predicted: float32 [3, 32, 32, 1024], P(None, 'stream', 'span', 'radial')
- wall_stress: float32 [2, 8192], P(None, ('stream', 'span', 'radial'))
Inputs may be any that keep to these rules, and one draw needn't show every extreme that they name: `slot_row`: for every tile, each of its exchange points 0 to 255 stands in exactly one slot of its 8 x 64 block; -1 marks an empty slot. In every draw some owner of each radial index has all 64 slots filled from every tile.
All inputs are finite; a program needn't handle non-finite values.
Results may differ from a plain program's by a relative error of at most 0.0003.
Values sent between devices are 32-bit elements; how exact they have to be, the bound alone decides.
A program may use at most 64 MiB of HBM per device.

v0:
```python
import jax
import jax.numpy as jnp
from jax import lax
from jax.sharding import PartitionSpec as P

ITERS = 6


source_gain = 0.00390625
relaxation = 0.8
time_step = 0.1
diffusion = 0.5
wall_gain = 0.25


def extended(block, sides, width):
    for axis, dim in sides:
        count = lax.axis_size(axis)
        forward = [(i, i + 1) for i in range(count - 1)]
        backward = [(target, source) for source, target in forward]
        low = lax.ppermute(
            lax.slice_in_dim(block, block.shape[dim] - width, None, axis=dim), axis, forward
        )
        high = lax.ppermute(lax.slice_in_dim(block, 0, width, axis=dim), axis, backward)
        block = jnp.concatenate([low, block, high], axis=dim)
    return block


def green_table(points):
    left_index = lax.broadcasted_iota(jnp.int32, (2 * points, 2 * points), 0)
    right_index = lax.broadcasted_iota(jnp.int32, (2 * points, 2 * points), 1)
    left_pos = left_index % points
    right_pos = right_index % points
    same_part = left_index // points == right_index // points
    values = (
        (jnp.minimum(left_pos, right_pos) + 1).astype(jnp.float32)
        * (points - jnp.maximum(left_pos, right_pos)).astype(jnp.float32)
        / (points + 1.0)
    )
    return jnp.where(same_part, values, jnp.zeros_like(values))


def wall_solve(samples, viscosity):
    points = samples.shape[1] // 2
    column = lax.broadcasted_iota(jnp.int32, samples.shape, 1)
    height = column % points
    at_wall = height == 0
    at_top = height == points - 1
    visc_above = jnp.where(at_top, viscosity, jnp.roll(viscosity, -1, axis=1))
    source_term = source_gain * samples + jnp.where(
        at_top, viscosity * samples, jnp.zeros_like(samples)
    )
    table = green_table(points)
    solution = jnp.zeros_like(samples)
    for sweep in range(ITERS):
        below_cell = jnp.where(at_wall, jnp.zeros_like(solution), jnp.roll(solution, 1, axis=1))
        above_cell = jnp.where(at_top, jnp.zeros_like(solution), jnp.roll(solution, -1, axis=1))
        applied = viscosity * (solution - below_cell) - visc_above * (above_cell - solution)
        solution = solution + relaxation * jnp.dot(
            source_term - applied,
            table,
            precision=lax.Precision.HIGHEST,
            preferred_element_type=jnp.float32,
        )
    wall_values = (points + 1.0) * viscosity * solution
    return jnp.stack([wall_values[:, 0], wall_values[:, points]], axis=1)


def fluid(padded):
    center = padded[:, 1:-1, 1:-1, 1:-1]
    upper_x = padded[:, 2:, 1:-1, 1:-1]
    lower_x = padded[:, :-2, 1:-1, 1:-1]
    upper_y = padded[:, 1:-1, 2:, 1:-1]
    lower_y = padded[:, 1:-1, :-2, 1:-1]
    upper_z = padded[:, 1:-1, 1:-1, 2:]
    lower_z = padded[:, 1:-1, 1:-1, :-2]
    divergence = 0.5 * (
        upper_x * upper_x[0:1]
        - lower_x * lower_x[0:1]
        + upper_y * upper_y[1:2]
        - lower_y * lower_y[1:2]
        + upper_z * upper_z[2:3]
        - lower_z * lower_z[2:3]
    )
    laplace = upper_x + lower_x + upper_y + lower_y + upper_z + lower_z - 6.0 * center
    return diffusion * laplace - divergence


def carry_profiles(payload):
    row_width = payload.shape[2]
    arrived = lax.all_to_all(payload, ("stream", "span"), split_axis=0, concat_axis=0, tiled=True)
    return arrived.reshape(-1, row_width)


def shards(velocity, probe, eddy, slot_row, row_cell):
    groups, capacity = slot_row.shape
    row_count, row_width = probe.shape
    cell_count = velocity.shape[1] * velocity.shape[2] * velocity.shape[3]
    flat_slots = slot_row.reshape(-1)
    occupied = flat_slots >= 0
    safe_rows = jnp.where(occupied, flat_slots, 0)
    target = jnp.where(occupied, flat_slots, row_count)
    padded = extended(velocity, (("stream", 1), ("span", 2), ("radial", 3)), 1)
    tendency = fluid(padded)
    outgoing = probe[safe_rows].reshape(groups, capacity, row_width)
    arrived = carry_profiles(outgoing)
    slot_stress = wall_solve(arrived, eddy)
    returned = lax.all_to_all(
        slot_stress.reshape(groups, capacity, 2),
        ("stream", "span"),
        split_axis=0,
        concat_axis=0,
        tiled=True,
    ).reshape(-1, 2)
    stress = jnp.zeros((row_count, 2), jnp.float32).at[target].set(returned, mode="drop")
    forcing = jnp.zeros((cell_count, 2), jnp.float32).at[row_cell].add(stress)
    forcing = jnp.transpose(forcing).reshape(
        2, velocity.shape[1], velocity.shape[2], velocity.shape[3]
    )
    predicted = velocity + time_step * tendency
    predicted = jnp.concatenate([predicted[0:2] - wall_gain * forcing, predicted[2:3]], axis=0)
    return (predicted, jnp.transpose(stress))


def solution(mesh):
    in_specs = (
        P(None, "stream", "span", "radial"),
        P(("stream", "span", "radial"), None),
        P(("stream", "span", "radial"), None),
        P(("stream", "span", "radial"), None),
        P(("stream", "span", "radial")),
    )
    out_specs = (P(None, "stream", "span", "radial"), P(None, ("stream", "span", "radial")))
    return jax.shard_map(shards, mesh=mesh, in_specs=in_specs, out_specs=out_specs, check_vma=False)
```

profile of v0, /device:TPU:2, one launch (start us, length us, event | category | flops | bytes accessed | tf_op | source)
XLA Modules:
  0.0 99.8 jit_solution(17554199306997575821)
XLA Ops:
  0.6 0.0 copy-start
  0.6 0.0 copy-start.1
  0.7 0.8 reshape.73
  1.5 0.6 compare_select_fusion.2
  2.1 1.6 %gather_fusion = f32[512,128]{1,0:T(8,128)} fusion(f32[256,128]{1,0:T(8,128)S(1)} %copy-done, s32[1024]{0:T(1024)S(1)} %pad_clamp_fusion), kind=kCustom, calls=%fused_computation | custom fusion | bytes 526336 | tf_op jit(solution)/shard_map/gather | solution.py:105
  3.7 5.8 %all-to-all-start = ((f32[8,64,128]{2,1,0:T(8,128)}), f32[8,64,128]{2,1,0:T(8,128)S(1)}, u32[]{:S(2)}, u32[]{:S(2)}) async-start(f32[8,64,128]{2,1,0:T(8,128)} %bitcast.8), calls=%async_computation | async-start | bytes 524288 | tf_op jit(solution)/shard_map/all_to_all | solution.py:91
  9.6 0.8 fusion.208
  10.4 3.9 %collective-permute-start.1 = (f32[3,1,16,256]{3,2,1,0:T(8,128)S(1)}, f32[3,1,16,256]{3,2,1,0:T(8,128)S(1)}, u32[]{:S(2)}, u32[]{:S(2)}) collective-permute-start(f32[3,1,16,256]{3,2,1,0:T(8,128)S(1)} %get-tuple-element.20), channel_id=1, source_target_pairs={{0,8},{8,16},{16,24},{1,9},{9,17},{17,25},{2,10},{10,18},{18,26},{... | collective-permute-start | bytes 147464 | tf_op jit(solution)/shard_map/ppermute | solution.py:21
  14.3 1.3 %collective-permute-start = (f32[3,1,16,256]{3,2,1,0:T(8,128)S(1)}, f32[3,1,16,256]{3,2,1,0:T(8,128)S(1)}, u32[]{:S(2)}, u32[]{:S(2)}) collective-permute-start(f32[3,1,16,256]{3,2,1,0:T(8,128)S(1)} %get-tuple-element.19), channel_id=1, source_target_pairs={{8,0},{16,8},{24,16},{9,1},{17,9},{25,17},{10,2},{18,10},{26,18},{... | collective-permute-start | bytes 147464 | tf_op jit(solution)/shard_map/ppermute | solution.py:24
  15.6 1.3 %compare_select_fusion.4 = s32[256]{0:T(256)} fusion(s32[256]{0:T(256)} %param.9), kind=kLoop, calls=%fused_computation.185 | loop fusion | flops 768 | bytes 2048 | tf_op jit(solution)/shard_map/select_n | solution.py:116
  16.9 1.1 %copy.51 = f32[512,128]{0,1:T(8,128)S(1)} copy(f32[512,128]{1,0:T(8,128)} %param.7) | data formatting | bytes 524288 | tf_op args[2]
  18.0 0.7 slice.214
  18.8 1.1 %constant_dynamic-update-slice_fusion.1 = (f32[3,9,16,256]{3,2,1,0:T(8,128)S(1)}, f32[3,9,16,256]{3,2,1,0:T(8,128)S(1)}, f32[3,10,16,256]{3,2,1,0:T(8,128)S(1)}) fusion(f32[3,8,16,256]{3,2,1,0:T(8,128)} %param.5, f32[3,9,16,256]{3,2,1,0:T(8,128)S(1)} %get-tuple-element.45, f32[3,10,16,256]{3,2,1,0:T(8,128)S(1)} %get-tuple-element.46), kind=kLoop, calls=%fused_computation.173 | loop fusion | bytes 1572864
  19.9 0.4 collective-permute-done
  20.4 1.3 %collective-permute-start.2 = (f32[3,10,1,256]{3,2,1,0:T(1,128)S(1)}, f32[3,10,1,256]{3,2,1,0:T(1,128)S(1)}, u32[]{:S(2)}, u32[]{:S(2)}) collective-permute-start(f32[3,10,1,256]{3,2,1,0:T(1,128)S(1)} %get-tuple-element.15), channel_id=1, source_target_pairs={{4,0},{5,1},{6,2},{7,3},{12,8},{13,9},{14,10},{15,11},{20,16},{21,... | collective-permute-start | bytes 92168 | tf_op jit(solution)/shard_map/ppermute | solution.py:24
  21.7 4.5 %collective-permute-start.3 = (f32[3,10,1,256]{3,2,1,0:T(1,128)S(1)}, f32[3,10,1,256]{3,2,1,0:T(1,128)S(1)}, u32[]{:S(2)}, u32[]{:S(2)}) collective-permute-start(f32[3,10,1,256]{3,2,1,0:T(1,128)S(1)} %get-tuple-element.14), channel_id=1, source_target_pairs={{0,4},{1,5},{2,6},{3,7},{8,12},{9,13},{10,14},{11,15},{16,20},{17,... | collective-permute-start | bytes 92168 | tf_op jit(solution)/shard_map/ppermute | solution.py:21
  26.2 0.7 slice_bitcast_fusion.1
  26.9 0.9 collective-permute-done.3
  27.8 0.1 pad_maximum_fusion
  27.9 0.2 fusion.206
  28.1 1.9 %collective-permute-start.4 = (f32[3,10,18,1]{3,2,1,0:T(8,128)S(1)}, f32[3,10,18,1]{3,2,1,0:T(8,128)S(1)}, u32[]{:S(2)}, u32[]{:S(2)}) collective-permute-start(f32[3,10,18,1]{3,2,1,0:T(8,128)S(1)} %get-tuple-element.8), channel_id=1, source_target_pairs={{1,0},{2,1},{3,2},{5,4},{6,5},{7,6},{9,8},{10,9},{11,10},{13,12},{... | collective-permute-start | bytes 6488 | tf_op jit(solution)/shard_map/ppermute | solution.py:24
  30.0 2.4 %collective-permute-start.5 = (f32[3,10,18,1]{3,2,1,0:T(8,128)S(1)}, f32[3,10,18,1]{3,2,1,0:T(8,128)S(1)}, u32[]{:S(2)}, u32[]{:S(2)}) collective-permute-start(f32[3,10,18,1]{3,2,1,0:T(8,128)S(1)} %get-tuple-element.9), channel_id=1, source_target_pairs={{0,1},{1,2},{2,3},{4,5},{5,6},{6,7},{8,9},{9,10},{10,11},{12,13},{... | collective-permute-start | bytes 6488 | tf_op jit(solution)/shard_map/ppermute | solution.py:21
  32.4 0.7 slice_bitcast_fusion
  33.1 1.9 %collective-permute-done.4 = f32[3,10,18,1]{3,2,1,0:T(8,128)S(1)} collective-permute-done((f32[3,10,18,1]{3,2,1,0:T(8,128)S(1)}, f32[3,10,18,1]{3,2,1,0:T(8,128)S(1)}, u32[]{:S(2)}, u32[]{:S(2)}) %collective-permute-start.4) | collective-permute-done | bytes 2192 | tf_op jit(solution)/shard_map/ppermute | solution.py:24
  35.0 3.8 %collective-permute-done.5 = f32[3,10,18,1]{3,2,1,0:T(8,128)S(1)} collective-permute-done((f32[3,10,18,1]{3,2,1,0:T(8,128)S(1)}, f32[3,10,18,1]{3,2,1,0:T(8,128)S(1)}, u32[]{:S(2)}, u32[]{:S(2)}) %collective-permute-start.5) | collective-permute-done | bytes 2192 | tf_op jit(solution)/shard_map/ppermute | solution.py:21
  38.8 0.8 fusion.100
  39.7 0.8 copy.52
  40.5 1.7 %convolution_multiply_fusion.5 = f32[512,128]{0,1:T(8,128)S(1)} fusion(f32[512,128]{0,1:T(8,128)S(1)} %copy.51, f32[128]{0:T(128)S(1)} %concatenate.78, s32[128]{0:T(128)S(1)} %get-tuple-element.52, s32[128]{0:T(128)S(1)} %get-tuple-element.54, pred[128]{0:T(512)(128)(4,1)S(1)} %get-tuple-element.50, s32[128]{0:T(128)S(1)} %get-tuple-element.51, ...), kind=kOutput, calls=%fused_computation.17 | convolution fusion | flops 101810176 | bytes 1051392 | tf_op jit(solution)/shard_map/dot_general | solution.py:59
  42.2 1.7 %fusion.7 = f32[512,128]{0,1:T(8,128)S(1)} fusion(f32[512,128]{0,1:T(8,128)S(1)} %convolution_multiply_fusion.5, f32[512,128]{0,1:T(8,128)S(1)} %copy.51, f32[512,127]{0,1:T(8,128)S(1)} %get-tuple-element.40, f32[512,1]{0,1:T(1,128)S(1)} %get-tuple-element.42, f32[512,1]{0,1:T(1,128)S(1)} %get-tuple-element.41, f32[512,127]{0,1:T(8,128)S(1)} %get-tuple-element.39, ...), kind=kOutput, calls=%fused_computation.16 | convolution fusion | flops 102268928 | bytes 1837312 | tf_op jit(solution)/shard_map/dot_general | solution.py:59
  44.0 1.7 %fusion.6 = f32[512,128]{0,1:T(8,128)S(1)} fusion(f32[512,128]{0,1:T(8,128)S(1)} %fusion.7, f32[512,128]{0,1:T(8,128)S(1)} %copy.51, f32[512,127]{0,1:T(8,128)S(1)} %get-tuple-element.36, f32[512,1]{0,1:T(1,128)S(1)} %get-tuple-element.38, f32[512,1]{0,1:T(1,128)S(1)} %get-tuple-element.37, f32[512,127]{0,1:T(8,128)S(1)} %get-tuple-element.35, ...), kind=kOutput, calls=%fused_computation.14 | convolution fusion | flops 102268928 | bytes 1837312 | tf_op jit(solution)/shard_map/dot_general | solution.py:59
  45.9 1.7 %fusion.5 = f32[512,128]{0,1:T(8,128)S(1)} fusion(f32[512,128]{0,1:T(8,128)S(1)} %fusion.6, f32[512,128]{0,1:T(8,128)S(1)} %copy.51, f32[512,127]{0,1:T(8,128)S(1)} %get-tuple-element.32, f32[512,1]{0,1:T(1,128)S(1)} %get-tuple-element.34, f32[512,1]{0,1:T(1,128)S(1)} %get-tuple-element.33, f32[512,127]{0,1:T(8,128)S(1)} %get-tuple-element.31, ...), kind=kOutput, calls=%fused_computation.12 | convolution fusion | flops 102268928 | bytes 1837312 | tf_op jit(solution)/shard_map/dot_general | solution.py:59
  47.7 1.7 %fusion.4 = f32[512,128]{0,1:T(8,128)S(1)} fusion(f32[512,128]{0,1:T(8,128)S(1)} %fusion.5, f32[512,128]{0,1:T(8,128)S(1)} %copy.51, f32[512,127]{0,1:T(8,128)S(1)} %get-tuple-element.28, f32[512,1]{0,1:T(1,128)S(1)} %get-tuple-element.30, f32[512,1]{0,1:T(1,128)S(1)} %get-tuple-element.29, f32[512,127]{0,1:T(8,128)S(1)} %get-tuple-element.27, ...), kind=kOutput, calls=%fused_computation.10 | convolution fusion | flops 102268928 | bytes 1837312 | tf_op jit(solution)/shard_map/dot_general | solution.py:59
  49.5 1.7 %fusion.3 = f32[512,128]{0,1:T(8,128)S(1)} fusion(f32[512,128]{0,1:T(8,128)S(1)} %fusion.4, f32[512,128]{0,1:T(8,128)S(1)} %copy.51, f32[512,127]{0,1:T(8,128)S(1)} %get-tuple-element.24, f32[512,1]{0,1:T(1,128)S(1)} %get-tuple-element.26, f32[512,1]{0,1:T(1,128)S(1)} %get-tuple-element.25, f32[512,127]{0,1:T(8,128)S(1)} %get-tuple-element.23, ...), kind=kOutput, calls=%fused_computation.8 | convolution fusion | flops 102400000 | bytes 1837312 | tf_op jit(solution)/shard_map/dot_general | solution.py:59
  51.2 0.1 reshape.76
  51.3 0.7 reshape.107
  52.0 7.1 %all-to-all-start.1 = ((f32[8,1,128]{2,1,0:T(1,128)}), f32[8,1,128]{2,1,0:T(1,128)S(1)}, u32[]{:S(2)}, u32[]{:S(2)}) async-start(f32[8,1,128]{2,1,0:T(1,128)} %reshape.107), calls=%async_computation.1 | async-start | bytes 8192 | tf_op jit(solution)/shard_map/all_to_all | solution.py:108
  59.1 1.8 %multiply_add_fusion = f32[3,8,16,256]{3,2,1,0:T(8,128)S(1)} fusion(f32[3,8,16,256]{3,2,1,0:T(8,128)S(1)} %copy-done.1, f32[3,10,1,256]{3,2,1,0:T(1,128)} %copy-done.2, f32[3,10,16,256]{3,2,1,0:T(8,128)S(1)} %get-tuple-element.44, f32[3,10,1,256]{3,2,1,0:T(1,128)} %copy-done.3, f32[3,10,18,1]{3,2,1,0:T(8,128)S(1)} %collective-permute-done.5, ...), kind=kLoop, calls=%fused_computation.28 | loop fusion | flops 3047424 | bytes 2916576 | tf_op jit(solution)/shard_map/add | solution.py:120
  60.9 4.6 %all-to-all-done.1 = f32[8,1,128]{2,1,0:T(1,128)S(1)} async-done(((f32[8,1,128]{2,1,0:T(1,128)}), f32[8,1,128]{2,1,0:T(1,128)S(1)}, u32[]{:S(2)}, u32[]{:S(2)}) %all-to-all-start.1) | async-done | bytes 4128 | tf_op jit(solution)/shard_map/all_to_all | solution.py:108
  65.5 0.5 broadcast.178
  66.0 0.7 reduce
  66.7 0.1 reshape.108
  66.8 0.2 copy.69
  66.9 1.9 %scatter_custom_fusion = f32[256,2]{1,0:T(8,128)S(1)} fusion(s32[512]{0:T(512)} %bitcast.34, f32[512,2]{1,0:T(8,128)S(1)} %bitcast.30, f32[]{:T(128)} %constant.76.clone.1), kind=kCustom, calls=%fused_computation.170 | custom fusion | bytes 2560 | tf_op jit(solution)/shard_map/scatter | solution.py:115
  68.8 8.3 %scatter_custom_fusion.1 = f32[32768,2]{1,0:T(8,128)} fusion(s32[256]{0:T(256)} %compare_select_fusion.4, f32[256,2]{1,0:T(8,128)S(1)} %scatter_custom_fusion, f32[]{:T(128)} %constant.76.clone.1), kind=kCustom, calls=%fused_computation.4 | custom fusion | flops 512 | bytes 262656 | tf_op jit(solution)/shard_map/scatter-add | solution.py:116
  77.1 11.3 %broadcast_multiply_fusion = f32[32768,2]{1,0:T(8,128)} fusion(f32[32768,2]{1,0:T(8,128)} %scatter_custom_fusion.1), kind=kLoop, calls=%fused_computation.3 | loop fusion | flops 65536 | bytes 524288 | tf_op jit(solution)/shard_map/mul | solution.py:121
  88.4 10.0 %copy.67 = f32[2,8,16,256]{3,2,1,0:T(8,128)S(1)} copy(f32[2,8,16,256]{0,3,2,1:T(8,128)} %bitcast.27) | data formatting | bytes 524288 | tf_op jit(solution)/shard_map/mul | solution.py:121
  98.4 0.7 copy.68
  99.0 0.8 pad_maximum_fusion.3
  (34 shorter events, 0.4 us)
Async XLA Ops:
  0.6 1.4 %copy-start = (f32[256,128]{1,0:T(8,128)S(1)}, f32[256,128]{1,0:T(8,128)}, u32[]{:S(2)}) copy-start(f32[256,128]{1,0:T(8,128)} %param.6) | copy-start | bytes 393220
  0.6 58.5 %copy-start.1 = (f32[3,8,16,256]{3,2,1,0:T(8,128)S(1)}, f32[3,8,16,256]{3,2,1,0:T(8,128)}, u32[]{:S(2)}) copy-start(f32[3,8,16,256]{3,2,1,0:T(8,128)} %param.5) | copy-start | bytes 1179652
  3.7 35.9 %all-to-all-start = ((f32[8,64,128]{2,1,0:T(8,128)}), f32[8,64,128]{2,1,0:T(8,128)S(1)}, u32[]{:S(2)}, u32[]{:S(2)}) async-start(f32[8,64,128]{2,1,0:T(8,128)} %bitcast.8), calls=%async_computation | async-start | bytes 524288 | tf_op jit(solution)/shard_map/all_to_all | solution.py:91
  10.4 8.4 %collective-permute-start.1 = (f32[3,1,16,256]{3,2,1,0:T(8,128)S(1)}, f32[3,1,16,256]{3,2,1,0:T(8,128)S(1)}, u32[]{:S(2)}, u32[]{:S(2)}) collective-permute-start(f32[3,1,16,256]{3,2,1,0:T(8,128)S(1)} %get-tuple-element.20), channel_id=1, source_target_pairs={{0,8},{8,16},{16,24},{1,9},{9,17},{17,25},{2,10},{10,18},{18,26},{... | collective-permute-start | bytes 147464 | tf_op jit(solution)/shard_map/ppermute | solution.py:21
  14.3 6.0 %collective-permute-start = (f32[3,1,16,256]{3,2,1,0:T(8,128)S(1)}, f32[3,1,16,256]{3,2,1,0:T(8,128)S(1)}, u32[]{:S(2)}, u32[]{:S(2)}) collective-permute-start(f32[3,1,16,256]{3,2,1,0:T(8,128)S(1)} %get-tuple-element.19), channel_id=1, source_target_pairs={{8,0},{16,8},{24,16},{9,1},{17,9},{25,17},{10,2},{18,10},{26,18},{... | collective-permute-start | bytes 147464 | tf_op jit(solution)/shard_map/ppermute | solution.py:24
  20.4 6.5 %collective-permute-start.2 = (f32[3,10,1,256]{3,2,1,0:T(1,128)S(1)}, f32[3,10,1,256]{3,2,1,0:T(1,128)S(1)}, u32[]{:S(2)}, u32[]{:S(2)}) collective-permute-start(f32[3,10,1,256]{3,2,1,0:T(1,128)S(1)} %get-tuple-element.15), channel_id=1, source_target_pairs={{4,0},{5,1},{6,2},{7,3},{12,8},{13,9},{14,10},{15,11},{20,16},{21,... | collective-permute-start | bytes 92168 | tf_op jit(solution)/shard_map/ppermute | solution.py:24
  21.7 6.1 %collective-permute-start.3 = (f32[3,10,1,256]{3,2,1,0:T(1,128)S(1)}, f32[3,10,1,256]{3,2,1,0:T(1,128)S(1)}, u32[]{:S(2)}, u32[]{:S(2)}) collective-permute-start(f32[3,10,1,256]{3,2,1,0:T(1,128)S(1)} %get-tuple-element.14), channel_id=1, source_target_pairs={{0,4},{1,5},{2,6},{3,7},{8,12},{9,13},{10,14},{11,15},{16,20},{17,... | collective-permute-start | bytes 92168 | tf_op jit(solution)/shard_map/ppermute | solution.py:21
  26.9 11.9 %copy-start.2 = (f32[3,10,1,256]{3,2,1,0:T(1,128)}, f32[3,10,1,256]{3,2,1,0:T(1,128)S(1)}, u32[]{:S(2)}) copy-start(f32[3,10,1,256]{3,2,1,0:T(1,128)S(1)} %collective-permute-done.2) | copy-start | bytes 92164
  27.8 11.0 %copy-start.3 = (f32[3,10,1,256]{3,2,1,0:T(1,128)}, f32[3,10,1,256]{3,2,1,0:T(1,128)S(1)}, u32[]{:S(2)}) copy-start(f32[3,10,1,256]{3,2,1,0:T(1,128)S(1)} %collective-permute-done.3) | copy-start | bytes 92164
  28.1 6.9 %collective-permute-start.4 = (f32[3,10,18,1]{3,2,1,0:T(8,128)S(1)}, f32[3,10,18,1]{3,2,1,0:T(8,128)S(1)}, u32[]{:S(2)}, u32[]{:S(2)}) collective-permute-start(f32[3,10,18,1]{3,2,1,0:T(8,128)S(1)} %get-tuple-element.8), channel_id=1, source_target_pairs={{1,0},{2,1},{3,2},{5,4},{6,5},{7,6},{9,8},{10,9},{11,10},{13,12},{... | collective-permute-start | bytes 6488 | tf_op jit(solution)/shard_map/ppermute | solution.py:24
  30.0 8.8 %collective-permute-start.5 = (f32[3,10,18,1]{3,2,1,0:T(8,128)S(1)}, f32[3,10,18,1]{3,2,1,0:T(8,128)S(1)}, u32[]{:S(2)}, u32[]{:S(2)}) collective-permute-start(f32[3,10,18,1]{3,2,1,0:T(8,128)S(1)} %get-tuple-element.9), channel_id=1, source_target_pairs={{0,1},{1,2},{2,3},{4,5},{5,6},{6,7},{8,9},{9,10},{10,11},{12,13},{... | collective-permute-start | bytes 6488 | tf_op jit(solution)/shard_map/ppermute | solution.py:21
  52.0 13.5 %all-to-all-start.1 = ((f32[8,1,128]{2,1,0:T(1,128)}), f32[8,1,128]{2,1,0:T(1,128)S(1)}, u32[]{:S(2)}, u32[]{:S(2)}) async-start(f32[8,1,128]{2,1,0:T(1,128)} %reshape.107), calls=%async_computation.1 | async-start | bytes 8192 | tf_op jit(solution)/shard_map/all_to_all | solution.py:108
where the time goes:
time: 101 us; the launch traced here: 99.8 us
  starting transfers between devices  28.3 us (28%)
  other arithmetic  25.6 us (25%)
  local copies, waits for them, and re-layouts  22.9 us (23%)
  waiting for transfers between devices  11.6 us (11%)
  matrix products  10.3 us (10%)
    mul x1, other arithmetic, shards(): wall_gain * forcing  11.3 us
    ppermute x3, starting transfers between devices, extended(): lax.ppermute(lax.slice_in_dim(block, block.shape[dim] - width, None, axis...  10.9 us
    dot_general x6, matrix products, wall_solve(): jnp.dot(source_term - applied, table, precision=lax.Precision.HIGHEST, pr...  10.3 us
    mul x1, local copies, waits for them, and re-layouts, shards(): wall_gain * forcing  9.95 us
    scatter-add x1, other arithmetic, shards(): forcing = jnp.zeros((cell_count, 2), jnp.float32).at[row_cell].add(stress)  8.31 us
    all_to_all x1, starting transfers between devices, shards(): lax.all_to_all(slot_stress.reshape(groups, capacity, 2), ('stream', 'span...  7.11 us
    all_to_all x1, starting transfers between devices, carry_profiles(): lax.all_to_all(payload, ('stream', 'span'), split_axis=0, concat_axis=0,...  5.83 us
    ppermute x3, waiting for transfers between devices, extended(): lax.ppermute(lax.slice_in_dim(block, block.shape[dim] - width, None, axis...  4.72 us
  transfers between devices with their start and end apart: 8, of which 5 were waited for; matrix products, arithmetic and copies ran while one was open for 9% of the time, Pallas kernels for 0%

commit v1 on v0

v1 whole, which is shorter than its diff:
```python
import functools
import jax
import jax.numpy as jnp
from jax import lax
from jax.experimental import pallas as pl
from jax.experimental.pallas import tpu as pltpu
from jax.sharding import PartitionSpec as P

ITERS = 6

source_gain = 0.00390625
relaxation = 0.8
time_step = 0.1
diffusion = 0.5
wall_gain = 0.25

MESH = pl.DeviceIdType.MESH


def halves(x):
    high = x.astype(jnp.bfloat16)
    return high, (x - high.astype(jnp.float32)).astype(jnp.bfloat16)


def dot(a, b, dims):
    return lax.dot_general(a, b, (dims, ((), ())), preferred_element_type=jnp.float32)


def suffix_sums(samples):
    width = samples.shape[1]
    points = width // 2
    row = lax.broadcasted_iota(jnp.int32, (width, width), 0)
    col = lax.broadcasted_iota(jnp.int32, (width, width), 1)
    keep = (col >= row) & ((col >= points) == (row >= points))
    table = jnp.where(keep, source_gain, 0.0).astype(jnp.bfloat16)
    high, low = halves(samples)
    return dot(table, high, ((1,), (1,))) + dot(table, low, ((1,), (1,)))


def wall_solve(visc, w):
    points, count = visc.shape[1], visc.shape[1] + 1
    v_top = visc[:, points - 1 : points]
    w_top = -(v_top * (w[:, points - 1 : points] * (1.0 / source_gain)))
    u, u_top = w, w_top
    d = jnp.zeros_like(w)
    d_top = jnp.zeros_like(w_top)
    for sweep in range(ITERS):
        mean = (jnp.sum(u, axis=1, keepdims=True) + u_top) * (1.0 / count)
        if sweep == ITERS - 1:
            first = d[:, 0:1] + relaxation * (u[:, 0:1] - mean)
            return (count * visc[:, 0:1] * first)[:, 0]
        d = d + relaxation * (u - mean)
        d_top = d_top + relaxation * (u_top - mean)
        u = w - visc * d
        u_top = w_top - v_top * d_top


def kernel(
    sizes, vel, probe_far, eddy, slots_far, cells_far, out, stress_out,
    vpad, recv, probe, slots, cells, y_out, y_in, z_out, z_in,
    send_sem, recv_sem, halo_send, halo_recv, local_sem,
):
    n_stream, n_span, n_radial = sizes
    s, p, r = (lax.axis_index(a) for a in ("stream", "span", "radial"))
    groups, capacity, width = eddy.shape
    _, cx, cy, cz = vel.shape
    me = s * n_span + p

    def partner(k):
        g = lax.rem(me + k, groups)
        return g, (lax.div(g, n_span), lax.rem(g, n_span), r)

    load = pltpu.make_async_copy(vel, vpad.at[:, pl.ds(1, cx)], local_sem.at[0])
    load.start()
    smalls = [
        pltpu.make_async_copy(far, near, local_sem.at[2 + i])
        for i, (far, near) in enumerate(((probe_far, probe), (slots_far, slots), (cells_far, cells)))
    ]
    for copy in smalls:
        copy.start()
    own = pltpu.make_async_copy(eddy.at[me], recv.at[me], local_sem.at[1])
    own.start()

    barrier = pltpu.get_barrier_semaphore()

    def greet(k, carry):
        pl.semaphore_signal(barrier, inc=1, device_id=partner(k)[1], device_id_type=MESH)
        return carry

    lax.fori_loop(1, groups, greet, 0)

    for radial in (lax.rem(r + 1, n_radial), lax.rem(r + n_radial - 1, n_radial)):
        pl.semaphore_signal(barrier, inc=1, device_id=(s, p, radial), device_id_type=MESH)
    pl.semaphore_wait(barrier, groups + 1)

    def eddy_copy(k):
        g, device = partner(k)
        return pltpu.make_async_remote_copy(
            src_ref=eddy.at[g], dst_ref=recv.at[me], send_sem=send_sem.at[g],
            recv_sem=recv_sem.at[me], device_id=device, device_id_type=MESH,
        )

    def send(k, carry):
        eddy_copy(k).start()
        return carry

    lax.fori_loop(1, groups, send, 0)

    load.wait()

    def faces():
        def copy(i, src, dst, device):
            return pltpu.make_async_remote_copy(
                src_ref=src, dst_ref=dst, send_sem=halo_send.at[i],
                recv_sem=halo_recv.at[i], device_id=device, device_id_type=MESH,
            )
        return [
            (s < n_stream - 1, s > 0, copy(0, vpad.at[:, cx], vpad.at[:, 0], (s + 1, p, r))),
            (s > 0, s < n_stream - 1, copy(1, vpad.at[:, 1], vpad.at[:, cx + 1], (s - 1, p, r))),
            (p < n_span - 1, p > 0, copy(2, y_out.at[0], y_in.at[0], (s, p + 1, r))),
            (p > 0, p < n_span - 1, copy(3, y_out.at[1], y_in.at[1], (s, p - 1, r))),
            (r < n_radial - 1, r > 0, copy(4, z_out.at[0], z_in.at[0], (s, p, r + 1))),
            (r > 0, r < n_radial - 1, copy(5, z_out.at[1], z_in.at[1], (s, p, r - 1))),
        ]

    sides = faces()
    fills = [vpad.at[:, 0], vpad.at[:, cx + 1], y_in.at[0], y_in.at[1], z_in.at[0], z_in.at[1]]
    for i in (0, 1):
        pl.when(sides[i][0])(sides[i][2].start)

    y_out[0] = vpad[:, 1 : cx + 1, cy - 1 : cy, :]
    y_out[1] = vpad[:, 1 : cx + 1, 0:1, :]
    for i in (2, 3):
        pl.when(sides[i][0])(sides[i][2].start)

    lanes = z_out.shape[2]
    shape4 = (3, cx, cy, lanes)
    plane = lax.broadcasted_iota(jnp.int32, shape4, 0) * cx + lax.broadcasted_iota(jnp.int32, shape4, 1)
    picked = plane == lax.broadcasted_iota(jnp.int32, shape4, 3)
    for i, column in ((0, cz - 1), (1, 0)):
        face = jnp.where(picked, vpad[:, 1 : cx + 1, :, column : column + 1], 0.0)
        z_out[i] = jnp.sum(jnp.sum(face, axis=0), axis=0)
    for i in (4, 5):
        pl.when(sides[i][0])(sides[i][2].start)

    for (_, arrives, _), ref in zip(sides, fills):
        @pl.when(jnp.logical_not(arrives))
        def _():
            ref[...] = jnp.zeros(ref.shape, ref.dtype)

    rows = probe.shape[0]
    for copy in smalls:
        copy.wait()
    w = suffix_sums(probe[...])
    if slots.shape[0] == 1:
        slot_line = slots[...]
    else:
        slot_line = jnp.concatenate([slots[g : g + 1, :] for g in range(groups)], axis=1)
    total = groups * capacity
    place = (lax.broadcasted_iota(jnp.int32, (rows, total), 0) == slot_line).astype(jnp.float32).astype(jnp.bfloat16)
    cell = cells[...]
    cell_z = lax.rem(cell, cz)
    cell_xy = lax.div(cell, cz)
    at_z = (lax.broadcasted_iota(jnp.int32, (cz, rows), 0) == cell_z).astype(jnp.float32).astype(jnp.bfloat16)

    for _, arrives, copy in sides:
        pl.when(arrives)(copy.wait_recv)

    line = lax.broadcasted_iota(jnp.int32, (3, cy, cz), 1)
    lane = lax.broadcasted_iota(jnp.int32, (3, cy, cz), 2)
    spot = lax.broadcasted_iota(jnp.int32, (3, cy, lanes), 0) * cx
    spot_lane = lax.broadcasted_iota(jnp.int32, (3, cy, lanes), 2)

    def step(x, carry):
        center = vpad[:, x + 1]
        lower_x = vpad[:, x]
        upper_x = vpad[:, x + 2]
        lower_y = jnp.where(line == 0, y_in[0, :, x], pltpu.roll(center, 1, 1))
        upper_y = jnp.where(line == cy - 1, y_in[1, :, x], pltpu.roll(center, cy - 1, 1))
        here = spot + x == spot_lane
        low_z = jnp.sum(jnp.where(here, z_in[0][None], 0.0), axis=2, keepdims=True)
        high_z = jnp.sum(jnp.where(here, z_in[1][None], 0.0), axis=2, keepdims=True)
        lower_z = jnp.where(lane == 0, low_z, pltpu.roll(center, 1, 2))
        upper_z = jnp.where(lane == cz - 1, high_z, pltpu.roll(center, cz - 1, 2))
        divergence = 0.5 * (
            upper_x * upper_x[0:1] - lower_x * lower_x[0:1]
            + upper_y * upper_y[1:2] - lower_y * lower_y[1:2]
            + upper_z * upper_z[2:3] - lower_z * lower_z[2:3]
        )
        laplace = upper_x + lower_x + upper_y + lower_y + upper_z + lower_z - 6.0 * center
        out[:, x] = center + time_step * (diffusion * laplace - divergence)
        return carry

    lax.fori_loop(0, cx, step, 0)

    own.wait()

    def arrived(k, carry):
        g, device = partner(k)
        pltpu.make_async_remote_copy(
            src_ref=eddy.at[g], dst_ref=recv.at[g], send_sem=send_sem.at[g],
            recv_sem=recv_sem.at[g], device_id=device, device_id_type=MESH,
        ).wait_recv()
        return carry

    lax.fori_loop(1, groups, arrived, 0)

    high, low = halves(recv[...].reshape(total, width))
    visc = dot(place, high, ((1,), (0,))) + dot(place, low, ((1,), (0,)))
    visc = jnp.transpose(visc).reshape(2, width // 2, rows)
    stress = wall_solve(visc, w.reshape(2, width // 2, rows))
    stress_out[...] = stress

    at_xy = lax.broadcasted_iota(jnp.int32, (cx * cy, rows), 0) == cell_xy
    for c in range(2):
        high, low = halves(jnp.where(at_xy, wall_gain * stress[c : c + 1], 0.0))
        forcing = dot(high, at_z, ((1,), (1,))) + dot(low, at_z, ((1,), (1,)))
        out[c] = out[c] - forcing.reshape(cx, cy, cz)

    for leaves, _, copy in sides:
        pl.when(leaves)(copy.wait_send)

    def sent(k, carry):
        eddy_copy(k).wait_send()
        return carry

    lax.fori_loop(1, groups, sent, 0)


def shards(sizes, velocity, probe, eddy, slot_row, row_cell):
    groups, capacity = slot_row.shape
    rows, width = probe.shape
    _, cx, cy, cz = velocity.shape
    if capacity % 8:
        slot_row = slot_row.reshape(1, groups * capacity)
    f32 = jnp.float32
    vmem = pl.BlockSpec(memory_space=pltpu.VMEM)
    hbm = pl.BlockSpec(memory_space=pltpu.HBM)
    return pl.pallas_call(
        functools.partial(kernel, sizes),
        out_shape=(
            jax.ShapeDtypeStruct(velocity.shape, f32),
            jax.ShapeDtypeStruct((2, rows), f32),
        ),
        in_specs=[hbm] * 5,
        out_specs=(vmem, vmem),
        scratch_shapes=[
            pltpu.VMEM((3, cx + 2, cy, cz), f32),
            pltpu.VMEM((groups, capacity, width), f32),
            pltpu.VMEM((rows, width), f32),
            pltpu.VMEM(slot_row.shape, jnp.int32),
            pltpu.VMEM((1, rows), jnp.int32),
            pltpu.VMEM((2, 3, cx, 1, cz), f32),
            pltpu.VMEM((2, 3, cx, 1, cz), f32),
            pltpu.VMEM((2, cy, 128), f32),
            pltpu.VMEM((2, cy, 128), f32),
            pltpu.SemaphoreType.DMA((groups,)),
            pltpu.SemaphoreType.DMA((groups,)),
            pltpu.SemaphoreType.DMA((6,)),
            pltpu.SemaphoreType.DMA((6,)),
            pltpu.SemaphoreType.DMA((5,)),
        ],
        compiler_params=pltpu.CompilerParams(
            collective_id=0, has_side_effects=True, vmem_limit_bytes=32 * 1024 * 1024
        ),
    )(velocity, probe, eddy.reshape(groups, capacity, width), slot_row, row_cell.reshape(1, rows))


def solution(mesh):
    in_specs = (
        P(None, "stream", "span", "radial"),
        P(("stream", "span", "radial"), None),
        P(("stream", "span", "radial"), None),
        P(("stream", "span", "radial"), None),
        P(("stream", "span", "radial")),
    )
    out_specs = (P(None, "stream", "span", "radial"), P(None, ("stream", "span", "radial")))
    sizes = tuple(mesh.shape[a] for a in ("stream", "span", "radial"))
    return jax.shard_map(
        functools.partial(shards, sizes), mesh=mesh, in_specs=in_specs, out_specs=out_specs, check_vma=False
    )
```

time: 101 us -> 21.3 us (0.21)
  the two profiles are of different devices: /device:TPU:2 before, /device:TPU:0 now
where the time goes in v1:
time: 21.3 us; the launch traced here: 21.1 us
  Pallas kernels  14.9 us (70%)
  local copies, waits for them, and re-layouts  5.53 us (26%)
  between operations  0.65 us (3%)
    pallas_call x1, Pallas kernels, shards(): pl.pallas_call(functools.partial(kernel, sizes), out_shape=(jax.ShapeDtyp...  14.9 us
    unnamed x12, local copies, waits for them, and re-layouts  5.53 us

profile of v1, /device:TPU:0, one launch (start us, length us, event | category | flops | bytes accessed | tf_op | source)
XLA Modules:
  0.0 21.1 jit_solution(11425435792831720485)
XLA Ops:
  0.6 0.0 copy-start.4
  0.6 0.7 %copy-done.4 = s32[256]{0:T(256)S(1)} copy-done((s32[256]{0:T(256)S(1)}, s32[256]{0:T(256)}, u32[]{:S(2)}) %copy-start.4) | copy-done | bytes 1048
  1.3 0.0 copy-start
  1.3 1.0 %copy-done = f32[3,8,16,256]{3,2,1,0:T(8,128)S(1)} copy-done((f32[3,8,16,256]{3,2,1,0:T(8,128)S(1)}, f32[3,8,16,256]{3,2,1,0:T(8,128)}, u32[]{:S(2)}) %copy-start) | copy-done | bytes 393240
  2.3 0.0 copy-start.1
  2.3 0.9 %copy-done.1 = f32[512,128]{1,0:T(8,128)S(1)} copy-done((f32[512,128]{1,0:T(8,128)S(1)}, f32[512,128]{1,0:T(8,128)}, u32[]{:S(2)}) %copy-start.1) | copy-done | bytes 262168
  3.3 0.0 copy-start.2
  3.3 0.9 %copy-done.2 = f32[256,128]{1,0:T(8,128)S(1)} copy-done((f32[256,128]{1,0:T(8,128)S(1)}, f32[256,128]{1,0:T(8,128)}, u32[]{:S(2)}) %copy-start.2) | copy-done | bytes 131096
  4.2 0.0 copy-start.3
  4.2 0.7 %copy-done.3 = s32[8,64]{1,0:T(8,128)S(1)} copy-done((s32[8,64]{1,0:T(8,128)S(1)}, s32[8,64]{1,0:T(8,128)}, u32[]{:S(2)}) %copy-start.3) | copy-done | bytes 2072
  4.8 14.9 %shard_map.68 = (f32[3,8,16,256]{3,2,1,0:T(8,128)S(1)}, f32[2,256]{1,0:T(2,128)S(1)}) custom-call(f32[3,8,16,256]{3,2,1,0:T(8,128)S(1)} %copy-done, f32[256,128]{1,0:T(8,128)S(1)} %copy-done.2, f32[8,64,128]{2,1,0:T(8,128)S(1)} %bitcast.2, s32[8,64]{1,0:T(8,128)S(1)} %copy-done.3, s32[1,256]{1,0:T(1,128)S(1)} %bitcast.3), custom_call_target="tpu_custom_call" | custom-call | tf_op jit(solution)/shard_map/pallas_call | solution.py:239
  19.7 0.7 %copy.9 = f32[3,8,16,256]{3,2,1,0:T(8,128)} copy(f32[3,8,16,256]{3,2,1,0:T(8,128)S(1)} %get-tuple-element.4) | data formatting | bytes 786432
  20.5 0.6 %copy.10 = f32[2,256]{1,0:T(2,128)} copy(f32[2,256]{1,0:T(2,128)S(1)} %get-tuple-element.5) | data formatting | bytes 4096
Async XLA Ops:
  0.6 0.7 %copy-start.4 = (s32[256]{0:T(256)S(1)}, s32[256]{0:T(256)}, u32[]{:S(2)}) copy-start(s32[256]{0:T(256)} %param.9) | copy-start | bytes 3076
  1.3 1.0 %copy-start = (f32[3,8,16,256]{3,2,1,0:T(8,128)S(1)}, f32[3,8,16,256]{3,2,1,0:T(8,128)}, u32[]{:S(2)}) copy-start(f32[3,8,16,256]{3,2,1,0:T(8,128)} %vel.1) | copy-start | bytes 1179652
  2.3 0.9 %copy-start.1 = (f32[512,128]{1,0:T(8,128)S(1)}, f32[512,128]{1,0:T(8,128)}, u32[]{:S(2)}) copy-start(f32[512,128]{1,0:T(8,128)} %param.7) | copy-start | bytes 786436
  3.3 0.9 %copy-start.2 = (f32[256,128]{1,0:T(8,128)S(1)}, f32[256,128]{1,0:T(8,128)}, u32[]{:S(2)}) copy-start(f32[256,128]{1,0:T(8,128)} %probe_far.1) | copy-start | bytes 393220
  4.2 0.7 %copy-start.3 = (s32[8,64]{1,0:T(8,128)S(1)}, s32[8,64]{1,0:T(8,128)}, u32[]{:S(2)}) copy-start(s32[8,64]{1,0:T(8,128)} %slots_far.1) | copy-start | bytes 6148

commit v2 on v1

--- a/solution.py
+++ b/solution.py
@@ -91,48 +91,9 @@
 
     for radial in (lax.rem(r + 1, n_radial), lax.rem(r + n_radial - 1, n_radial)):
         pl.semaphore_signal(barrier, inc=1, device_id=(s, p, radial), device_id_type=MESH)
-    pl.semaphore_wait(barrier, groups + 1)
-
-    def eddy_copy(k):
-        g, device = partner(k)
-        return pltpu.make_async_remote_copy(
-            src_ref=eddy.at[g], dst_ref=recv.at[me], send_sem=send_sem.at[g],
-            recv_sem=recv_sem.at[me], device_id=device, device_id_type=MESH,
-        )
-
-    def send(k, carry):
-        eddy_copy(k).start()
-        return carry
-
-    lax.fori_loop(1, groups, send, 0)
-
     load.wait()
-
-    def faces():
-        def copy(i, src, dst, device):
-            return pltpu.make_async_remote_copy(
-                src_ref=src, dst_ref=dst, send_sem=halo_send.at[i],
-                recv_sem=halo_recv.at[i], device_id=device, device_id_type=MESH,
-            )
-        return [
-            (s < n_stream - 1, s > 0, copy(0, vpad.at[:, cx], vpad.at[:, 0], (s + 1, p, r))),
-            (s > 0, s < n_stream - 1, copy(1, vpad.at[:, 1], vpad.at[:, cx + 1], (s - 1, p, r))),
-            (p < n_span - 1, p > 0, copy(2, y_out.at[0], y_in.at[0], (s, p + 1, r))),
-            (p > 0, p < n_span - 1, copy(3, y_out.at[1], y_in.at[1], (s, p - 1, r))),
-            (r < n_radial - 1, r > 0, copy(4, z_out.at[0], z_in.at[0], (s, p, r + 1))),
-            (r > 0, r < n_radial - 1, copy(5, z_out.at[1], z_in.at[1], (s, p, r - 1))),
-        ]
-
-    sides = faces()
-    fills = [vpad.at[:, 0], vpad.at[:, cx + 1], y_in.at[0], y_in.at[1], z_in.at[0], z_in.at[1]]
-    for i in (0, 1):
-        pl.when(sides[i][0])(sides[i][2].start)
-
     y_out[0] = vpad[:, 1 : cx + 1, cy - 1 : cy, :]
     y_out[1] = vpad[:, 1 : cx + 1, 0:1, :]
-    for i in (2, 3):
-        pl.when(sides[i][0])(sides[i][2].start)
-
     lanes = z_out.shape[2]
     shape4 = (3, cx, cy, lanes)
     plane = lax.broadcasted_iota(jnp.int32, shape4, 0) * cx + lax.broadcasted_iota(jnp.int32, shape4, 1)
@@ -140,13 +101,43 @@
     for i, column in ((0, cz - 1), (1, 0)):
         face = jnp.where(picked, vpad[:, 1 : cx + 1, :, column : column + 1], 0.0)
         z_out[i] = jnp.sum(jnp.sum(face, axis=0), axis=0)
-    for i in (4, 5):
-        pl.when(sides[i][0])(sides[i][2].start)
-
-    for (_, arrives, _), ref in zip(sides, fills):
+
+    def face_copy(i, src, dst, device):
+        return pltpu.make_async_remote_copy(
+            src_ref=src, dst_ref=dst, send_sem=halo_send.at[i],
+            recv_sem=halo_recv.at[i], device_id=device, device_id_type=MESH,
+        )
+
+    sides = [
+        (s < n_stream - 1, s > 0, face_copy(0, vpad.at[:, cx], vpad.at[:, 0], (s + 1, p, r)), vpad.at[:, 0]),
+        (s > 0, s < n_stream - 1, face_copy(1, vpad.at[:, 1], vpad.at[:, cx + 1], (s - 1, p, r)), vpad.at[:, cx + 1]),
+        (p < n_span - 1, p > 0, face_copy(2, y_out.at[0], y_in.at[0], (s, p + 1, r)), y_in.at[0]),
+        (p > 0, p < n_span - 1, face_copy(3, y_out.at[1], y_in.at[1], (s, p - 1, r)), y_in.at[1]),
+        (r < n_radial - 1, r > 0, face_copy(4, z_out.at[0], z_in.at[0], (s, p, r + 1)), z_in.at[0]),
+        (r > 0, r < n_radial - 1, face_copy(5, z_out.at[1], z_in.at[1], (s, p, r - 1)), z_in.at[1]),
+    ]
+    for _, arrives, _, ref in sides:
         @pl.when(jnp.logical_not(arrives))
         def _():
             ref[...] = jnp.zeros(ref.shape, ref.dtype)
+
+    pl.semaphore_wait(barrier, groups + 1)
+
+    def eddy_copy(k):
+        g, device = partner(k)
+        return pltpu.make_async_remote_copy(
+            src_ref=eddy.at[g], dst_ref=recv.at[me], send_sem=send_sem.at[g],
+            recv_sem=recv_sem.at[me], device_id=device, device_id_type=MESH,
+        )
+
+    def send(k, carry):
+        eddy_copy(k).start()
+        return carry
+
+    lax.fori_loop(1, groups, send, 0)
+
+    for leaves, _, copy, _ in sides:
+        pl.when(leaves)(copy.start)
 
     rows = probe.shape[0]
     for copy in smalls:
@@ -163,7 +154,7 @@
     cell_xy = lax.div(cell, cz)
     at_z = (lax.broadcasted_iota(jnp.int32, (cz, rows), 0) == cell_z).astype(jnp.float32).astype(jnp.bfloat16)
 
-    for _, arrives, copy in sides:
+    for _, arrives, copy, _ in sides:
         pl.when(arrives)(copy.wait_recv)
 
     line = lax.broadcasted_iota(jnp.int32, (3, cy, cz), 1)
@@ -217,7 +208,7 @@
         forcing = dot(high, at_z, ((1,), (1,))) + dot(low, at_z, ((1,), (1,)))
         out[c] = out[c] - forcing.reshape(cx, cy, cz)
 
-    for leaves, _, copy in sides:
+    for leaves, _, copy, _ in sides:
         pl.when(leaves)(copy.wait_send)
 
     def sent(k, carry):
@@ -261,7 +252,7 @@
             pltpu.SemaphoreType.DMA((5,)),
         ],
         compiler_params=pltpu.CompilerParams(
-            collective_id=0, has_side_effects=True, vmem_limit_bytes=32 * 1024 * 1024
+            collective_id=0, has_side_effects=True
         ),
     )(velocity, probe, eddy.reshape(groups, capacity, width), slot_row, row_cell.reshape(1, rows))
 

time: 21.3 us -> 18.7 us (0.88)
  local copies, waits for them, and re-layouts: 5.53 us -> 2.35 us
  Pallas kernels: 14.9 us -> 15.6 us
    unnamed x12 -> x4, local copies, waits for them, and re-layouts: 5.53 us -> 2.35 us
    pallas_call x1, Pallas kernels: 14.9 us -> 15.6 us  [shards(): pl.pallas_call(functools.partial(kernel, sizes), out_shape=(jax.ShapeDtyp...]
where the time goes in v2:
time: 18.7 us; the launch traced here: 18.6 us
  Pallas kernels  15.6 us (83%)
  local copies, waits for them, and re-layouts  2.35 us (13%)
  between operations  0.65 us (3%)
    pallas_call x1, Pallas kernels, shards(): pl.pallas_call(functools.partial(kernel, sizes), out_shape=(jax.ShapeDtyp...  15.6 us
    unnamed x4, local copies, waits for them, and re-layouts  2.35 us

profile of v2, /device:TPU:0, one launch (start us, length us, event | category | flops | bytes accessed | tf_op | source)
XLA Modules:
  0.0 18.6 jit_solution(275037140608403169)
XLA Ops:
  0.6 15.6 %shard_map.68 = (f32[3,8,16,256]{3,2,1,0:T(8,128)}, f32[2,256]{1,0:T(2,128)}) custom-call(f32[3,8,16,256]{3,2,1,0:T(8,128)} %vel.1, f32[256,128]{1,0:T(8,128)} %probe_far.1, f32[8,64,128]{2,1,0:T(8,128)} %bitcast.2, s32[8,64]{1,0:T(8,128)} %slots_far.1, s32[1,256]{1,0:T(1,128)} %bitcast.3), custom_call_target="tpu_custom_call" | custom-call | tf_op jit(solution)/shard_map/pallas_call | solution.py:230
  16.2 0.0 copy-start
  16.2 1.8 %copy.9 = f32[3,8,16,256]{3,2,1,0:T(8,128)} copy(f32[3,8,16,256]{3,2,1,0:T(8,128)} %get-tuple-element.4) | data formatting | bytes 786432
  18.0 0.0 copy-done
  18.0 0.6 %copy.10 = f32[2,256]{1,0:T(2,128)} copy(f32[2,256]{1,0:T(2,128)S(1)} %copy-done) | data formatting | bytes 4096
Async XLA Ops:
  16.2 1.8 %copy-start = (f32[2,256]{1,0:T(2,128)S(1)}, f32[2,256]{1,0:T(2,128)}, u32[]{:S(2)}) copy-start(f32[2,256]{1,0:T(2,128)} %get-tuple-element.5) | copy-start | bytes 6148

commit v3 on v2

--- a/solution.py
+++ b/solution.py
@@ -230,8 +230,8 @@
     return pl.pallas_call(
         functools.partial(kernel, sizes),
         out_shape=(
-            jax.ShapeDtypeStruct(velocity.shape, f32),
-            jax.ShapeDtypeStruct((2, rows), f32),
+            pltpu.VMEM(velocity.shape, f32),
+            pltpu.VMEM((2, rows), f32),
         ),
         in_specs=[hbm] * 5,
         out_specs=(vmem, vmem),

time: 18.7 us -> 16.9 us (0.904)
  local copies, waits for them, and re-layouts: 2.35 us -> 1.33 us
  Pallas kernels: 15.6 us -> 14.8 us
    unnamed x4 -> x2, local copies, waits for them, and re-layouts: 2.35 us -> 1.33 us
    pallas_call x1, Pallas kernels: 15.6 us -> 14.8 us  [shards(): pl.pallas_call(functools.partial(kernel, sizes), out_shape=(pltpu.VMEM(ve...]
where the time goes in v3:
time: 16.9 us; the launch traced here: 16.8 us
  Pallas kernels  14.8 us (88%)
  local copies, waits for them, and re-layouts  1.33 us (8%)
  between operations  0.64 us (4%)
    pallas_call x1, Pallas kernels, shards(): pl.pallas_call(functools.partial(kernel, sizes), out_shape=(pltpu.VMEM(ve...  14.8 us
    unnamed x2, local copies, waits for them, and re-layouts  1.33 us

profile of v3, /device:TPU:0, one launch (start us, length us, event | category | flops | bytes accessed | tf_op | source)
XLA Modules:
  0.0 16.8 jit_solution(17379036294081792831)
XLA Ops:
  0.6 14.8 %shard_map.68 = (f32[3,8,16,256]{3,2,1,0:T(8,128)S(1)}, f32[2,256]{1,0:T(2,128)S(1)}) custom-call(f32[3,8,16,256]{3,2,1,0:T(8,128)} %vel.1, f32[256,128]{1,0:T(8,128)} %probe_far.1, f32[8,64,128]{2,1,0:T(8,128)} %bitcast.2, s32[8,64]{1,0:T(8,128)} %slots_far.1, s32[1,256]{1,0:T(1,128)} %bitcast.3), custom_call_target="tpu_custom_call" | custom-call | tf_op jit(solution)/shard_map/pallas_call | solution.py:230
  15.5 0.7 %copy.9 = f32[3,8,16,256]{3,2,1,0:T(8,128)} copy(f32[3,8,16,256]{3,2,1,0:T(8,128)S(1)} %get-tuple-element.2) | data formatting | bytes 786432
  16.2 0.6 %copy.10 = f32[2,256]{1,0:T(2,128)} copy(f32[2,256]{1,0:T(2,128)S(1)} %get-tuple-element.3) | data formatting | bytes 4096

commit v4 on v3

--- a/solution.py
+++ b/solution.py
@@ -134,9 +134,10 @@
         eddy_copy(k).start()
         return carry
 
+    for leaves, _, copy, _ in sides[2:]:
+        pl.when(leaves)(copy.start)
     lax.fori_loop(1, groups, send, 0)
-
-    for leaves, _, copy, _ in sides:
+    for leaves, _, copy, _ in sides[:2]:
         pl.when(leaves)(copy.start)
 
     rows = probe.shape[0]
@@ -154,7 +155,7 @@
     cell_xy = lax.div(cell, cz)
     at_z = (lax.broadcasted_iota(jnp.int32, (cz, rows), 0) == cell_z).astype(jnp.float32).astype(jnp.bfloat16)
 
-    for _, arrives, copy, _ in sides:
+    for _, arrives, copy, _ in sides[2:]:
         pl.when(arrives)(copy.wait_recv)
 
     line = lax.broadcasted_iota(jnp.int32, (3, cy, cz), 1)
@@ -182,7 +183,10 @@
         out[:, x] = center + time_step * (diffusion * laplace - divergence)
         return carry
 
-    lax.fori_loop(0, cx, step, 0)
+    lax.fori_loop(1, cx - 1, step, 0)
+    for _, arrives, copy, _ in sides[:2]:
+        pl.when(arrives)(copy.wait_recv)
+    lax.fori_loop(0, 2, lambda i, carry: step(i * (cx - 1), carry), 0)
 
     own.wait()
 
@@ -216,6 +220,17 @@
         return carry
 
     lax.fori_loop(1, groups, sent, 0)
+
+
+def write_out(first, second, first_out, second_out, sem):
+    copies = [
+        pltpu.make_async_copy(first, first_out, sem.at[0]),
+        pltpu.make_async_copy(second, second_out, sem.at[1]),
+    ]
+    for copy in copies:
+        copy.start()
+    for copy in copies:
+        copy.wait()
 
 
 def shards(sizes, velocity, probe, eddy, slot_row, row_cell):
@@ -227,7 +242,7 @@
     f32 = jnp.float32
     vmem = pl.BlockSpec(memory_space=pltpu.VMEM)
     hbm = pl.BlockSpec(memory_space=pltpu.HBM)
-    return pl.pallas_call(
+    results = pl.pallas_call(
         functools.partial(kernel, sizes),
         out_shape=(
             pltpu.VMEM(velocity.shape, f32),
@@ -255,6 +270,17 @@
             collective_id=0, has_side_effects=True
         ),
     )(velocity, probe, eddy.reshape(groups, capacity, width), slot_row, row_cell.reshape(1, rows))
+    return pl.pallas_call(
+        write_out,
+        out_shape=(
+            jax.ShapeDtypeStruct(velocity.shape, f32),
+            jax.ShapeDtypeStruct((2, rows), f32),
+        ),
+        in_specs=[pl.BlockSpec(memory_space=pl.ANY)] * 2,
+        out_specs=(hbm, hbm),
+        scratch_shapes=[pltpu.SemaphoreType.DMA((2,))],
+        compiler_params=pltpu.CompilerParams(vmem_limit_bytes=2 * 1024 * 1024),
+    )(*results)
 
 
 def solution(mesh):

time: 16.9 us -> 15.6 us (0.923)
  local copies, waits for them, and re-layouts: 1.33 us -> 0 us
    unnamed x2 -> x0, local copies, waits for them, and re-layouts: 1.33 us -> none
    pallas_call x1, Pallas kernels: 14.8 us -> 14 us  [shards(): pl.pallas_call(functools.partial(kernel, sizes), out_shape=(pltpu.VMEM(ve...]
    pallas_call x0 -> x1, Pallas kernels: none -> 0.77 us  [shards(): pl.pallas_call(write_out, out_shape=(jax.ShapeDtypeStruct(velocity.shape,...]
where the time goes in v4:
time: 15.6 us; the launch traced here: 15.4 us
  Pallas kernels  14.8 us (95%)
  between operations  0.64 us (4%)
    pallas_call x1, Pallas kernels, shards(): pl.pallas_call(functools.partial(kernel, sizes), out_shape=(pltpu.VMEM(ve...  14 us
    pallas_call x1, Pallas kernels, shards(): pl.pallas_call(write_out, out_shape=(jax.ShapeDtypeStruct(velocity.shape,...  0.77 us

profile of v4, /device:TPU:0, one launch (start us, length us, event | category | flops | bytes accessed | tf_op | source)
XLA Modules:
  0.0 15.4 jit_solution(315673695248669036)
XLA Ops:
  0.6 14.0 %shard_map.68 = (f32[3,8,16,256]{3,2,1,0:T(8,128)S(1)}, f32[2,256]{1,0:T(2,128)S(1)}) custom-call(f32[3,8,16,256]{3,2,1,0:T(8,128)} %vel.1, f32[256,128]{1,0:T(8,128)} %probe_far.1, f32[8,64,128]{2,1,0:T(8,128)} %bitcast.2, s32[8,64]{1,0:T(8,128)} %slots_far.1, s32[1,256]{1,0:T(1,128)} %bitcast.3), custom_call_target="tpu_custom_call" | custom-call | tf_op jit(solution)/shard_map/pallas_call | solution.py:245
  14.7 0.8 %shard_map.69 = (f32[3,8,16,256]{3,2,1,0:T(8,128)}, f32[2,256]{1,0:T(2,128)}) custom-call(f32[3,8,16,256]{3,2,1,0:T(8,128)S(1)} %get-tuple-element.4.first, f32[2,256]{1,0:T(2,128)S(1)} %get-tuple-element.5.second), custom_call_target="tpu_custom_call" | custom-call | tf_op jit(solution)/shard_map/pallas_call | solution.py:273

commit v5 on v4

--- a/solution.py
+++ b/solution.py
@@ -121,25 +121,6 @@
         def _():
             ref[...] = jnp.zeros(ref.shape, ref.dtype)
 
-    pl.semaphore_wait(barrier, groups + 1)
-
-    def eddy_copy(k):
-        g, device = partner(k)
-        return pltpu.make_async_remote_copy(
-            src_ref=eddy.at[g], dst_ref=recv.at[me], send_sem=send_sem.at[g],
-            recv_sem=recv_sem.at[me], device_id=device, device_id_type=MESH,
-        )
-
-    def send(k, carry):
-        eddy_copy(k).start()
-        return carry
-
-    for leaves, _, copy, _ in sides[2:]:
-        pl.when(leaves)(copy.start)
-    lax.fori_loop(1, groups, send, 0)
-    for leaves, _, copy, _ in sides[:2]:
-        pl.when(leaves)(copy.start)
-
     rows = probe.shape[0]
     for copy in smalls:
         copy.wait()
@@ -154,6 +135,29 @@
     cell_z = lax.rem(cell, cz)
     cell_xy = lax.div(cell, cz)
     at_z = (lax.broadcasted_iota(jnp.int32, (cz, rows), 0) == cell_z).astype(jnp.float32).astype(jnp.bfloat16)
+
+    pl.semaphore_wait(barrier, groups + 1)
+
+    def eddy_copy(k):
+        g, device = partner(k)
+        return pltpu.make_async_remote_copy(
+            src_ref=eddy.at[g], dst_ref=recv.at[me], send_sem=send_sem.at[g],
+            recv_sem=recv_sem.at[me], device_id=device, device_id_type=MESH,
+        )
+
+    def send(k, carry):
+        eddy_copy(k).start()
+        return carry
+
+    for leaves, _, copy, _ in sides[2:]:
+        pl.when(leaves)(copy.start)
+    if groups == 8:
+        for k in (2, 1, 3, 4, 6, 5, 7):
+            send(k, 0)
+    else:
+        lax.fori_loop(1, groups, send, 0)
+    for leaves, _, copy, _ in sides[:2]:
+        pl.when(leaves)(copy.start)
 
     for _, arrives, copy, _ in sides[2:]:
         pl.when(arrives)(copy.wait_recv)

time: 15.6 us -> 15.2 us (0.974)
  Pallas kernels: 14.8 us -> 14.4 us
    pallas_call x1, Pallas kernels: 14 us -> 13.7 us  [shards(): pl.pallas_call(functools.partial(kernel, sizes), out_shape=(pltpu.VMEM(ve...]
where the time goes in v5:
time: 15.2 us; the launch traced here: 15.1 us
  Pallas kernels  14.4 us (95%)
  between operations  0.64 us (4%)
    pallas_call x1, Pallas kernels, shards(): pl.pallas_call(functools.partial(kernel, sizes), out_shape=(pltpu.VMEM(ve...  13.7 us
    pallas_call x1, Pallas kernels, shards(): pl.pallas_call(write_out, out_shape=(jax.ShapeDtypeStruct(velocity.shape,...  0.77 us

profile of v5, /device:TPU:0, one launch (start us, length us, event | category | flops | bytes accessed | tf_op | source)
XLA Modules:
  0.0 15.1 jit_solution(8679243181608508373)
XLA Ops:
  0.6 13.7 %shard_map.68 = (f32[3,8,16,256]{3,2,1,0:T(8,128)S(1)}, f32[2,256]{1,0:T(2,128)S(1)}) custom-call(f32[3,8,16,256]{3,2,1,0:T(8,128)} %vel.1, f32[256,128]{1,0:T(8,128)} %probe_far.1, f32[8,64,128]{2,1,0:T(8,128)} %bitcast.2, s32[8,64]{1,0:T(8,128)} %slots_far.1, s32[1,256]{1,0:T(1,128)} %bitcast.3), custom_call_target="tpu_custom_call" | custom-call | tf_op jit(solution)/shard_map/pallas_call | solution.py:249
  14.3 0.8 %shard_map.69 = (f32[3,8,16,256]{3,2,1,0:T(8,128)}, f32[2,256]{1,0:T(2,128)}) custom-call(f32[3,8,16,256]{3,2,1,0:T(8,128)S(1)} %get-tuple-element.4.first, f32[2,256]{1,0:T(2,128)S(1)} %get-tuple-element.5.second), custom_call_target="tpu_custom_call" | custom-call | tf_op jit(solution)/shard_map/pallas_call | solution.py:277
